TPU v7x, 32 devices: a whole 2x2x4 slice. The times are simulated.
32 devices in a mesh: dp: 16 (over z, y, core), fsdp: 2 (over x).
Axes of the slice: x: 2, y: 2, z: 4, core: 2. Of those that a mesh axis runs over, the one named last changes fastest.
Arguments:
- frames_in: bfloat16 [16, 1024, 1024], P('dp', 'fsdp'), may hold values from -6 to 6
- prefix_len: int32 [16], P('dp'), may hold values from 1 to 512, as said below
- w_qkv: bfloat16 [1024, 3072], P(('dp', 'fsdp')), may hold values from -0.1875 to 0.1875
- w_out: bfloat16 [1024, 1024], P(('dp', 'fsdp')), may hold values from -1.5 to 1.5
- w_up: bfloat16 [1024, 4096], P(('dp', 'fsdp')), may hold values from -0.1875 to 0.1875
- w_down: bfloat16 [4096, 1024], P(('dp', 'fsdp')), may hold values from -0.09375 to 0.09375
- gains: bfloat16 [2, 1024], P(None, ('dp', 'fsdp')), may hold values from 0.25 to 1.75
- shifts: bfloat16 [2, 1024], P(None, ('dp', 'fsdp')), may hold values from -1.796875 to 1.796875
- cotangent: bfloat16 [16, 1024, 1024], P('dp', 'fsdp'), may hold values from -6 to 6
Outputs:
- frames_out: bfloat16 [16, 1024, 1024], P('dp', 'fsdp')
- grad_in: float32 [16, 1024, 1024], P('dp', 'fsdp')
- grad_qkv: float32 [1024, 3072], P(('dp', 'fsdp'))
- grad_out: float32 [1024, 1024], P(('dp', 'fsdp'))
- grad_up: float32 [1024, 4096], P(('dp', 'fsdp'))
- grad_down: float32 [4096, 1024], P(('dp', 'fsdp'))
- grad_gains: float32 [2, 1024], P(None, ('dp', 'fsdp'))
- grad_shifts: float32 [2, 1024], P(None, ('dp', 'fsdp'))
Inputs may be any that keep to these rules, and one draw needn't show every extreme that they name: `prefix_len`: some item's prefix has exactly 512 frames.
All inputs are finite; a program needn't handle non-finite values.
Results may differ from a plain program's by a relative error of at most 0.011.
Values may be sent and summed in bfloat16 or wider, within the bound.
A program may use at most 256 MiB of HBM per device.

v0:
```python
import functools
import math

import jax
import jax.numpy as jnp
from jax import lax
from jax.experimental import pallas as pl
from jax.experimental.pallas import tpu as pltpu
from jax.sharding import PartitionSpec as P

H = 16
HD = 64
EPS = 1e-05
BF = jnp.bfloat16
F32 = jnp.float32
LOG2E = math.log2(math.e)
SCALE2 = 0.125 * LOG2E
PAIR = 2 * HD
TILE = 512
MESH = pl.DeviceIdType.MESH
DMA = pltpu.SemaphoreType.DMA
VMEM_LIMIT = 60 * 2**20


def coords():
    dp, f = lax.axis_index("dp"), lax.axis_index("fsdp")
    q = lax.div(dp, 2)
    return lax.div(q, 2), lax.rem(q, 2), lax.rem(dp, 2), f


def dev(z, y, c, f):
    return ((z * 2 + y) * 2 + c, f)


def remote(src, dst, send, recv, device):
    return pltpu.make_async_remote_copy(
        src_ref=src, dst_ref=dst, send_sem=send, recv_sem=recv, device_id=device, device_id_type=MESH
    )


def greet(peers):
    barrier = pltpu.get_barrier_semaphore()
    for peer in peers:
        pl.semaphore_signal(barrier, inc=1, device_id=peer, device_id_type=MESH)
    pl.semaphore_wait(barrier, len(peers))


def all_peers(nz, z, y, c, f):
    peers = [dev(lax.rem(z + k, nz), y, c, f) for k in range(1, nz)]
    return peers + [dev(z, 1 - y, c, f), dev(z, y, c, 1 - f), dev(z, y, 1 - c, f)]


def dot_nn(a, b):
    return lax.dot_general(a, b, (((1,), (0,)), ((), ())), preferred_element_type=F32)


def dot_nt(a, b):
    return lax.dot_general(a, b, (((1,), (1,)), ((), ())), preferred_element_type=F32)


def dot_tn(a, b):
    return lax.dot_general(a, b, (((0,), (0,)), ((), ())), preferred_element_type=F32)


def normalise(v):
    center = v - jnp.mean(v, -1, keepdims=True)
    scale = lax.rsqrt(jnp.mean(center * center, -1, keepdims=True) + EPS)
    return center * scale, scale


def lane_half():
    return lax.broadcasted_iota(jnp.int32, (1, PAIR), 1) // HD


def fill_bias(bias, prefix, c, transposed):
    rows = bias.shape[0]
    step = 64

    def body(j, part):
        a = lax.broadcasted_iota(jnp.int32, (step, rows), 0) + j * step
        b = lax.broadcasted_iota(jnp.int32, (step, rows), 1)
        row, key = (b, a) if transposed else (a, b)
        bias[part, :] = jnp.where((key <= row) | (key + c * rows < prefix), 0.0, -1e30)

    tiles(rows // step, step, body)


def norm_back(gh, n, scale, gain):
    gn = gh * gain
    return scale * (gn - jnp.mean(gn, -1, keepdims=True) - n * jnp.mean(gn * n, -1, keepdims=True))


class Gather:
    def __init__(self, nz, place, shards, outs, chunks, sems):
        self.nz, self.place, self.shards, self.outs, self.chunks = nz, place, shards, outs, chunks
        self.send, self.recv, self.own = sems

    @staticmethod
    def sem_shapes(n):
        return [DMA((n, 12)), DMA((n, 12)), DMA((n,))]

    def mine(self, i):
        w, r0, r, c0, n = self.chunks[i]
        return self.shards[w].at[pl.ds(r0, r), pl.ds(c0, n)]

    def at(self, i, *where):
        w, r0, r, c0, n = self.chunks[i]
        where += (slice(None),) * (4 - len(where))
        return self.outs[w].at[where + (pl.ds(r0, r), pl.ds(c0, n))]

    def hop(self, i, slot, src, dst, device):
        return remote(src, dst, self.send.at[i, slot], self.recv.at[i, slot], device)

    def copies(self, i):
        z, y, c, f = self.place
        nz = self.nz
        every = slice(None)
        core, xp, yp = dev(z, y, 1 - c, f), dev(z, y, c, 1 - f), dev(z, 1 - y, c, f)
        mine, home = self.mine(i), self.at(i, z, y, c, f)

        def same(slot, ref, device):
            return self.hop(i, slot, ref, ref, device)

        zs = [dev(lax.rem(z + k, nz), y, c, f) for k in range(1, nz)]
        line = self.at(i, every, y, c, f)
        other = self.at(i, every, 1 - y, c, f)
        zero = {
            0: [self.hop(i, k, mine, home, zs[k]) for k in range(nz - 1)],
            1: [same(3, line, yp), same(4, line, xp), same(8, line, core)],
            2: [same(5, other, xp), same(9, other, core)],
            3: [same(10, self.at(i, every, every, c, 1 - f), core)],
        }
        rows = self.at(i, z, y, c)
        plane = self.at(i, every, y, c)
        one = {
            0: [self.hop(i, 3, mine, home, xp)],
            1: [same(k, rows, zs[k]) for k in range(nz - 1)],
            2: [same(4, plane, yp), same(8, plane, core)],
            3: [same(9, self.at(i, every, 1 - y, c), core)],
        }
        return zero, one

    def arrivals(self, i):
        z, y, c, f = self.place
        nz = self.nz
        every = slice(None)
        zk = [lax.rem(z + nz - k, nz) for k in range(1, nz)]
        core = dev(z, y, 1 - c, f)

        def here(slot, *where):
            ref = self.at(i, *where)
            return self.hop(i, slot, ref, ref, core)

        zero = {
            1: [here(k, zk[k], y, c, f) for k in range(nz - 1)],
            2: [here(3, every, 1 - y, c, f)],
            3: [here(4, every, y, c, 1 - f), here(5, every, 1 - y, c, 1 - f)],
            4: [here(8, every, y, 1 - c), here(9, every, 1 - y, 1 - c)],
        }
        one = {
            1: [here(3, z, y, c, 1 - f)],
            2: [here(k, zk[k], y, c) for k in range(nz - 1)],
            3: [here(4, every, 1 - y, c)],
            4: [here(8, every, y, 1 - c, f), here(9, every, 1 - y, 1 - c, f), here(10, every, every, 1 - c, 1 - f)],
        }
        return zero, one

    def local(self, i):
        z, y, c, f = self.place
        return pltpu.make_async_copy(self.mine(i), self.at(i, z, y, c, f), self.own.at[i])

    def stage(self, i, s):
        if s == 1:
            self.local(i).wait()
        for core in range(2):

            @pl.when(self.place[2] == core)
            def _():
                if s:
                    for copy in self.arrivals(i)[core][s]:
                        copy.wait_recv()
                if s < 4:
                    for copy in self.copies(i)[core][s]:
                        copy.start()

    def tick(self, t):
        for s in range(4):
            if 0 <= t - s < len(self.chunks):
                self.stage(t - s, s)

    def finish(self, i):
        for core in range(2):

            @pl.when(self.place[2] == core)
            def _():
                for copies in self.copies(i)[core].values():
                    for copy in copies:
                        copy.wait_send()


RING = 6
BLOCK = 32
WIDE = 1024


def tiles(count, size, body, hooks=None):
    @pl.loop(0, count)
    def _(j):
        body(j, pl.ds(pl.multiple_of(j * size, size), size))
        run_hooks(j, hooks)


def run_hooks(j, hooks):
    for at, hook in (hooks or {}).items():

        @pl.when(j == at)
        def _():
            hook()


def flat(ref, cols):
    v = ref[:, :, :, :, cols]
    return v.reshape(math.prod(v.shape[:-1]), v.shape[-1])


def add_blocks(dst, parts, out=None):
    lead, n = dst.shape[:-2], dst.shape[-1]
    size = min(n, 256)

    @pl.loop(0, math.prod(lead) * (n // size))
    def _(j):
        cols = pl.ds(pl.multiple_of(lax.rem(j, n // size) * size, size), size)
        at, rest = [], lax.div(j, n // size)
        for count in reversed(lead):
            at.insert(0, lax.rem(rest, count))
            rest = lax.div(rest, count)
        at = tuple(at) + (slice(None), cols)
        total = dst[at].astype(F32)
        for p in parts:
            total = total + p[at].astype(F32)
        if out is None:
            dst[at] = total.astype(dst.dtype)
        else:
            out[at] = total


class Scatter:
    def __init__(self, nz, place, sums, second, third, outs, sems):
        self.nz, self.place, self.sums, self.second, self.third = nz, place, sums, second, third
        self.outs, self.done = outs, set()
        self.send, self.recv, self.free = sems

    @staticmethod
    def sem_shapes(n):
        return [DMA((n, 5)), DMA((n, 5)), pltpu.SemaphoreType.REGULAR((RING,))]

    def peers(self):
        z, y, c, f = self.place
        zs = [dev(lax.rem(z + k, self.nz), y, c, f) for k in range(1, self.nz)]
        return zs, dev(z, 1 - y, c, f), dev(z, y, c, 1 - f)

    def hop(self, i, slot, src, dst, device):
        return remote(src, dst, self.send.at[i, slot], self.recv.at[i, slot], device)

    def copies(self, i):
        z, y, c, f = self.place
        s, b2, b3, nz = self.sums[i], self.second[i], self.third[i], self.nz
        zs, yp, xp = self.peers()
        zt = [lax.rem(z + k, nz) for k in range(1, nz)]
        zero = {
            0: [self.hop(i, 0, s.at[:, :, 1 - f], b2, xp)],
            1: [self.hop(i, 1, s.at[:, 1 - y, f], b3.at[pl.ds(0, nz)], yp)],
            2: [self.hop(i, 2 + k, s.at[zt[k], y, f], b3.at[nz + k], zs[k]) for k in range(nz - 1)],
        }
        one = {
            0: [self.hop(i, 0, s.at[:, 1 - y], b2, yp)],
            1: [self.hop(i, 1 + k, s.at[zt[k], y], b3.at[pl.ds(2 * k, 2)], zs[k]) for k in range(nz - 1)],
            2: [self.hop(i, nz, s.at[z, y, 1 - f], b3.at[2 * (nz - 1)], xp)],
        }
        return zero, one

    def stage(self, i, st):
        z, y, c, f = self.place
        nz = self.nz
        self.done.add((i, st))
        s, b2, b3 = self.sums[i], self.second[i], self.third[i]
        copies = self.copies(i)
        zs, yp, xp = self.peers()
        ringed = i < len(self.sums) - 1
        if st == 0 and ringed and i >= RING:
            pl.semaphore_wait(self.free.at[i % RING], nz + 1)

        @pl.when(c == 0)
        def _():
            if st:
                for copy in copies[0][st - 1]:
                    copy.wait_recv()
            if st == 0:
                copies[0][0][0].start()
            if st == 1:
                add_blocks(s.at[:, 1 - y, f], [b2.at[:, 1 - y]])
                copies[0][1][0].start()
                add_blocks(s.at[:, y, f], [b2.at[:, y]])
            if st == 2:
                for k in range(nz - 1):
                    zt = lax.rem(z + k + 1, nz)
                    add_blocks(s.at[zt, y, f], [b3.at[zt]])
                    copies[0][2][k].start()
                add_blocks(s.at[z, y, f], [b3.at[z]])
            if st == 3:
                add_blocks(s.at[z, y, f], [b3.at[nz + k] for k in range(nz - 1)], self.outs[i])

        @pl.when(c == 1)
        def _():
            if st:
                for copy in copies[1][st - 1]:
                    copy.wait_recv()
            if st == 0:
                copies[1][0][0].start()
            if st == 1:
                for k in range(nz - 1):
                    zt = lax.rem(z + k + 1, nz)
                    add_blocks(s.at[zt, y], [b2.at[zt]])
                    copies[1][1][k].start()
                add_blocks(s.at[z, y], [b2.at[z]])
            if st == 2:
                add_blocks(s.at[z, y, 1 - f], [b3.at[2 * k + 1 - f] for k in range(nz - 1)])
                copies[1][2][0].start()
                add_blocks(s.at[z, y, f], [b3.at[2 * k + f] for k in range(nz - 1)])
            if st == 3:
                add_blocks(s.at[z, y, f], [b3.at[2 * (nz - 1)]], self.outs[i])

        if st == 3 and ringed and i + RING < len(self.sums) - 1:
            for peer in zs + [yp, xp]:
                pl.semaphore_signal(self.free.at[i % RING], inc=1, device_id=peer, device_id_type=MESH)

    def tick(self, t):
        for st in range(1, 4):
            i = t - st
            if (i, st - 1) in self.done and (i, st) not in self.done:
                self.stage(i, st)

    def finish(self, i):
        for core in range(2):

            @pl.when(self.place[2] == core)
            def _():
                for copies in self.copies(i)[core].values():
                    for copy in copies:
                        copy.wait_send()


class Producer:
    def __init__(self, place, buf, land, sems):
        self.place, self.buf, self.land = place, buf, land
        self.send, self.recv, self.credit = sems
        z, y, c, f = place
        self.core = dev(z, y, 1 - c, f)
        self.made, self.pending = 0, None

    def copy(self, slot):
        theirs = self.buf.at[slot, :, 1 - self.place[2]]
        return remote(theirs, self.land.at[slot], self.send.at[slot], self.recv.at[slot], self.core)

    def before(self, slot):
        self.copy(slot).wait_send()
        pl.semaphore_wait(self.credit.at[slot], 1)

    def absorb(self, j, target):
        c = self.place[2]
        slot = lax.rem(j, 2)
        self.copy(slot).wait_recv()
        for i in range(4):
            ref = target(j, i)
            for k in range(2):
                ref[k] = (self.buf[slot, i, c, k].astype(F32) + self.land[slot, i, k].astype(F32)).astype(BF)
        pl.semaphore_signal(self.credit.at[slot], inc=1, device_id=self.core, device_id_type=MESH)

    def flush(self):
        if self.pending is not None:
            self.absorb(*self.pending)
            self.pending = None

    def run(self, count, product, where, target, hooks=None):
        fresh, pending = self.made == 0, self.pending

        @pl.loop(0, count)
        def _(j):
            slot = lax.rem(j, 2)
            if not fresh:
                self.before(slot)
            elif count > 2:

                @pl.when(j >= 2)
                def _():
                    self.before(slot)

            v = product(j)
            for i in range(4):
                for k in range(2):
                    for core in range(2):
                        at = where(i, core, k)
                        self.buf[slot, i, core, k] = v[at : at + BLOCK].astype(BF)
            self.copy(slot).start()
            if pending is not None:

                @pl.when(j == 0)
                def _():
                    self.absorb(*pending)

            @pl.when(j >= 1)
            def _():
                self.absorb(j - 1, target)

            run_hooks(j, hooks)

        self.made += count
        self.pending = (count - 1, target)

    def finish(self):
        for slot in range(2):
            self.before(slot)


def row_blocks(i, core, k):
    return BLOCK * (4 * i + 2 * core + k)


def deep_blocks(i, core, k):
    return BLOCK * (8 * core + 4 * k + i)


def attend_forward(c, qkv, cross, bias, att, lse, hooks):
    rows, d = att.shape
    half = lane_half()
    lane = lax.broadcasted_iota(jnp.int32, (1, PAIR), 1)
    rt = rows // 2

    def one(q, blocks):
        scores = []
        for keys, _, extra in blocks:
            s = dot_nt(q, keys) * SCALE2
            scores.append(s if extra is None else s + extra)
        peak = functools.reduce(jnp.maximum, [jnp.max(s, -1, keepdims=True) for s in scores])
        total = None
        for s, (_, values, _) in zip(scores, blocks):
            part = dot_nn(jnp.exp2(s - peak).astype(BF), values)
            total = part if total is None else total + part
        return total, peak

    def pair(p, second):
        cols = pl.ds(pl.multiple_of(p * PAIR, PAIR), PAIR)
        kcols = pl.ds(pl.multiple_of(d + p * PAIR, PAIR), PAIR)
        vcols = pl.ds(pl.multiple_of(2 * d + p * PAIR, PAIR), PAIR)
        def half_rows(r, part):
            results = []
            for h in range(2):
                mine = half == h
                q = jnp.where(mine, qkv[part, cols], 0.0).astype(BF)

                def val(v):
                    return jnp.where(mine, v, 1.0).astype(BF)

                if second:
                    blocks = [(cross[:, cols], val(cross[:, kcols]), None)]
                    if r > 0:
                        blocks.append((qkv[pl.ds(0, rt), kcols], val(qkv[pl.ds(0, rt), vcols]), None))
                    blocks.append((qkv[part, kcols], val(qkv[part, vcols]), bias[part, pl.ds(r * rt, rt)]))
                else:
                    blocks = [(qkv[:, kcols], val(qkv[:, vcols]), bias[part, :])]
                total, peak = one(q, blocks)
                sums = pltpu.roll(total, HD, axis=1)
                results.append(total / sums)
                both = jnp.where(mine, sums, total)
                lse[part, :] = jnp.where(lane == 2 * p + h, peak + jnp.log2(both), lse[part, :])
            att[part, cols] = jnp.where(half == 0, results[0], results[1]).astype(BF)

        if second:
            for r in range(2):
                half_rows(r, pl.ds(r * rt, rt))
        else:
            tiles(2, rt, half_rows)

    @pl.loop(0, d // PAIR)
    def _(p):
        for second in range(2):

            @pl.when(c == second)
            def _():
                pair(p, second == 1)

        run_hooks(p, hooks)


SHARED = 5


def attend_backward(c, qkv, cross, biast, lset, deltat, far_lse, far_delta, go, gq, gq2, more, hooks):
    rows, d = go.shape
    half = lane_half()
    rt = rows // 2
    pairs = d // PAIR

    def term(p, keys, values, krows, qrows, queries, grads, lse, delta, masked, total):
        gk = gv = None
        for h in range(2):
            mine = half == h
            q = jnp.where(mine, queries, 0.0).astype(BF)
            g = jnp.where(mine, grads, 0.0).astype(BF)
            km = jnp.where(mine, keys, 0.0).astype(BF)
            s = dot_nt(keys, q) * SCALE2
            if masked:
                s = s + biast[krows, qrows]
            pr = jnp.exp2(s - lse[pl.ds(2 * p + h, 1), qrows])
            gs = (pr * (dot_nt(values, g) - delta[pl.ds(2 * p + h, 1), qrows])).astype(BF)
            k1, v1 = dot_nn(gs, q), dot_nn(pr.astype(BF), g)
            gk, gv = (k1, v1) if gk is None else (gk + k1, gv + v1)
            total[qrows, :] = total[qrows, :] + dot_tn(gs, km)
        return gk, gv

    every = pl.ds(0, rows)
    first, last = pl.ds(0, PAIR), pl.ds(PAIR, PAIR)

    @pl.loop(0, pairs)
    def _(i):
        @pl.when(c == 0)
        def _():
            heavy = i < pairs - SHARED
            p = lax.rem(i + SHARED, pairs)
            cols = pl.ds(pl.multiple_of(p * PAIR, PAIR), PAIR)
            kcols = pl.ds(pl.multiple_of(d + p * PAIR, PAIR), PAIR)
            vcols = pl.ds(pl.multiple_of(2 * d + p * PAIR, PAIR), PAIR)
            gq[...] = jnp.zeros_like(gq)

            @pl.when(heavy)
            def _():
                gq2[...] = jnp.zeros_like(gq2)

                def far_part(r, krows):
                    more[krows, first], more[krows, last] = term(
                        p, qkv[krows, kcols], qkv[krows, vcols], krows, every, cross[:, cols], cross[:, kcols], far_lse, far_delta, False, gq2
                    )

                tiles(2, rt, far_part)
                cross[:, cols] = (gq2[...] * 0.125).astype(BF)

            @pl.when(i == pairs - SHARED)
            def _():
                more[:, first] = jnp.zeros_like(gq)
                more[:, last] = jnp.zeros_like(gq)

            def own_part(r, krows):
                gk, gv = term(
                    p, qkv[krows, kcols], qkv[krows, vcols], krows, every, qkv[:, cols], go[:, cols], lset, deltat, True, gq
                )
                qkv[krows, kcols] = ((gk + more[krows, first]) * 0.125).astype(BF)
                qkv[krows, vcols] = (gv + more[krows, last]).astype(BF)

            tiles(2, rt, own_part)
            qkv[:, cols] = (gq[...] * 0.125).astype(BF)

        @pl.when(c == 1)
        def _():
            p = i
            cols = pl.ds(pl.multiple_of(p * PAIR, PAIR), PAIR)
            kcols = pl.ds(pl.multiple_of(d + p * PAIR, PAIR), PAIR)
            vcols = pl.ds(pl.multiple_of(2 * d + p * PAIR, PAIR), PAIR)
            gq[...] = jnp.zeros_like(gq)

            @pl.when(p < SHARED)
            def _():
                def near_part(r, krows):
                    gk, gv = term(
                        p, cross[krows, cols], cross[krows, kcols], krows, every, qkv[:, cols], go[:, cols], lset, deltat, False, gq
                    )
                    cross[krows, cols] = (gk * 0.125).astype(BF)
                    cross[krows, kcols] = gv.astype(BF)

                tiles(2, rt, near_part)

            for r in range(2):
                krows, qrows = pl.ds(r * rt, rt), pl.ds(r * rt, rows - r * rt)
                gk, gv = term(
                    p, qkv[krows, kcols], qkv[krows, vcols], krows, qrows, qkv[qrows, cols], go[qrows, cols], lset, deltat, True, gq
                )
                qkv[krows, kcols] = (gk * 0.125).astype(BF)
                qkv[krows, vcols] = gv.astype(BF)
            qkv[:, cols] = (gq[...] * 0.125).astype(BF)

        run_hooks(i, hooks)


def layer_kernel(nz, *refs):
    (
        frames_in, cot_in, pre_in, s_qkv, s_out, s_up, s_down, s_par,
        fo, gi, gl, f_qkv, f_out, f_up, f_down, f_par, g_qkv, g_out, g_up, g_down, g_par,
        x, cot, pre, h1, qkv, cross, att, x1, h2, a, gp, wa, wb, gh, gz, go, bias, narrow, narrow2, lset, deltat, far_lse, far_delta,
        acc, par, parv, ht, buf, land, sdown, spar, ptheirs, pland, second, third, psecond, pthird,
        ag_send, ag_recv, ag_own, rs_send, rs_recv, rs_free, p_send, p_recv, p_credit,
        load_sem, swap_sem, io_sem, io_recv,
    ) = refs
    place = z, y, c, f = coords()
    rows, d = x.shape
    ff = a.shape[-1]
    core, far = dev(z, y, 1 - c, f), dev(z, y, 1 - c, 1 - f)
    straight = c == f
    nk = d // WIDE

    chunks = [(4, 0, 16, 0, PAIR)]
    chunks += [(0, 0, BLOCK, d + h * TILE, TILE) for h in range(2)] + [(0, 0, BLOCK, b * d, d) for b in (2, 0)]
    chunks += [(1, 0, BLOCK, 0, d)]
    chunks += [(2, 0, BLOCK, k * WIDE, WIDE) for k in range(ff // WIDE)]
    down_rows = [(0, BLOCK), (BLOCK, BLOCK), (2 * BLOCK, BLOCK), (3 * BLOCK, BLOCK // 2), (7 * BLOCK // 2, BLOCK // 2)]
    chunks += [(3, r0, r, 0, d) for r0, r in down_rows]
    ag = Gather(nz, place, (s_qkv, s_out, s_up, s_down, s_par), (f_qkv, f_out, f_up, f_down, f_par), chunks, (ag_send, ag_recv, ag_own))

    ups, downs = ff // WIDE, 4
    sums = [sdown.at[k] for k in range(downs)]
    sums += [a.at[:, :, :, :, pl.ds(k * WIDE, WIDE)] for k in range(ups)]
    tail = [(3 * d, d), (d, d), (2 * d, d), (0, TILE), (TILE, TILE)]
    sums += [gp.at[:, :, :, :, pl.ds(c0, w)] for c0, w in tail]
    goes = [g_down.at[pl.ds(k * BLOCK, BLOCK)] for k in range(downs)]
    goes += [g_up.at[:, pl.ds(k * WIDE, WIDE)] for k in range(ups)]
    goes += [g_out] + [g_qkv.at[:, pl.ds(c0, w)] for c0, w in tail[1:]]
    n = len(sums)
    widths = [WIDE] * (downs + ups) + [w for _, w in tail]
    rs = Scatter(
        nz, place, sums + [spar], [second.at[i % RING, :, :, :, pl.ds(0, widths[i])] for i in range(n)] + [psecond],
        [third.at[i % RING, :, :, pl.ds(0, widths[i])] for i in range(n)] + [pthird], goes + [g_par], (rs_send, rs_recv, rs_free),
    )
    maker = Producer(place, buf, land, (p_send, p_recv, p_credit))

    for i in range(len(chunks)):
        ag.local(i).start()
    greet(all_peers(nz, *place) + [far])

    swaps = []
    quarter = rows // 4
    quarters = [pl.ds(i * quarter, quarter) for i in range(4)]
    moves = [(pre_in, pre)]
    moves += [(cot_in.at[q], cot.at[q]) for q in quarters] + [(frames_in.at[q], x.at[q]) for q in quarters]
    for i, (src, dst) in enumerate(moves):
        swaps.append((pltpu.make_async_copy(src, dst, swap_sem.at[i, 0]), remote(src, dst, swap_sem.at[i, 1], swap_sem.at[i, 2], far)))

    def swap_start(i):
        @pl.when(straight)
        def _():
            swaps[i][0].start()

        @pl.when(jnp.logical_not(straight))
        def _():
            swaps[i][1].start()

    def swap_wait(i):
        @pl.when(straight)
        def _():
            swaps[i][0].wait()

        @pl.when(jnp.logical_not(straight))
        def _():
            swaps[i][1].wait()

    def between(i, src, dst):
        return remote(src, dst, swap_sem.at[i, 1], swap_sem.at[i, 2], core)

    def ag_tick(t):
        return lambda: ag.tick(t)

    def rs_tick(t):
        return lambda: rs.tick(t)

    def rs_begin(i):
        return lambda: rs.stage(i, 0)

    def small(b):
        return pl.ds(b * BLOCK, BLOCK)

    def load(i, src, dst):
        return pltpu.make_async_copy(src, dst, load_sem.at[i])

    def load_block(i, b):
        if b == 3:
            return load(i, f_out, wa.at[:, :, :, :, small(3)])
        return load(i, f_qkv.at[:, :, :, :, :, pl.ds(b * d, d)], wa.at[:, :, :, :, small(b)])

    def block(b, at=slice(None)):
        v = wa[at, :, :, :, small(b)]
        return v.reshape(math.prod(v.shape[:-1]), d)

    ag.stage(0, 0)
    ag.stage(1, 0)
    swap_start(0)
    swap_start(5)
    ag.stage(0, 1)
    ag.tick(2)
    swap_start(6)
    ag.tick(3)
    swap_start(7)
    ag.stage(0, 4)
    get_par = load(0, f_par, parv)
    get_par.start()
    swap_wait(0)
    fill_bias(bias, pre[0:1, 0:1], c, False)
    get_par.wait()
    for t in range(d // PAIR):
        total = None
        for k in range(4):
            piece = parv[t // 2, t % 2, k // 2, k % 2].astype(F32)
            total = piece if total is None else total + piece
        par[:, pl.ds(t * PAIR, PAIR)] = total
    step = 64

    def norm_one(j, part):
        nrm, _ = normalise(x[part, :].astype(F32))
        h1[part, :] = (nrm * par[0:1, :] + par[2:3, :]).astype(BF)

    ag.tick(4)
    swap_start(8)
    for i in range(4):
        swap_wait(5 + i)
    tiles(rows // step, step, norm_one)
    keyvals = between(14, qkv.at[:, pl.ds(d, 2 * d)], cross)
    ag.stage(1, 4)
    for i, b in enumerate((1, 2, 0)):
        ag.tick(5 + i)
        ag.stage(2 + i, 4)
        get = load_block(1 + i, b)
        get.start()
        get.wait()
        for t in range(d // TILE):
            cols = pl.ds(t * TILE, TILE)
            w = wa[:, :, :, :, small(b), cols].reshape(d, TILE)
            qkv[:, pl.ds(b * d + t * TILE, TILE)] = dot_nn(h1[...], w).astype(BF)
        swap_start(1 + i)
        if b == 2:

            @pl.when(c == 0)
            def _():
                keyvals.start()

    @pl.when(c == 1)
    def _():
        keyvals.wait_recv()

    swap_start(4)
    narrow[...] = jnp.zeros_like(narrow)
    attend_forward(c, qkv, cross, bias, att, narrow, {1: ag_tick(8), 6: ag_tick(9)})
    ag.stage(5, 4)
    get_out = load_block(4, 3)
    get_out.start()

    @pl.when(c == 0)
    def _():
        keyvals.wait_send()

    lset[...] = narrow[...].T[:H, :]

    def get_up(k):
        return load(5 + k, f_up.at[:, :, :, :, :, pl.ds(k * WIDE, WIDE)], wb.at[:, :, :, :, :, pl.ds(k * WIDE, WIDE)])

    ag.stage(6, 4)
    get_up(0).start()
    get_out.wait()
    for t in range(d // TILE):
        cols = pl.ds(t * TILE, TILE)
        w = wa[:, :, :, :, small(3), cols].reshape(d, TILE)
        x1[:, cols] = x[:, cols].astype(F32) + dot_nn(att[...], w)
    ag.tick(10)

    def norm_two(j, part):
        nrm, _ = normalise(x1[part, :])
        h2[part, :] = (nrm * par[1:2, :] + par[3:4, :]).astype(BF)

    tiles(rows // step, step, norm_two)
    u = gh.at[:, pl.ds(0, TILE)]

    def up(cols):
        gh[:, pl.ds(0, TILE)] = dot_nn(h2[...], wb[:, :, :, :, :, cols].reshape(d, TILE))

        @pl.loop(0, rows // BLOCK)
        def _(j):
            at = (lax.div(j, 4), lax.rem(lax.div(j, 2), 2), lax.rem(j, 2), slice(None), cols)
            v = gh[pl.ds(pl.multiple_of(j * BLOCK, BLOCK), BLOCK), pl.ds(0, TILE)]
            phi = 0.5 * (1.0 + lax.erf(v * math.sqrt(0.5)))
            dens = jnp.exp2(v * v * (-0.5 * LOG2E)) * (1.0 / math.sqrt(2.0 * math.pi))
            a[at] = (v * phi).astype(BF)
            gp[at] = (phi + v * dens).astype(BF)

    for i in range(4):
        swap_wait(1 + i)

    def down_product(j):
        for k in range(ups):

            @pl.when(j == 2 * k)
            def _():
                if k:
                    ag.stage(6 + k, 4)
                    get_up(k).start()
                get_up(k).wait()

        cols = pl.ds(pl.multiple_of(j * TILE, TILE), TILE)
        up(cols)
        for k in range(ups):

            @pl.when(j == 2 * k + 1)
            def _():
                ag.tick(11 + k)

        return dot_tn(flat(a, cols), cot[...])

    maker.run(2 * ups, down_product, deep_blocks, lambda j, i: sdown.at[i, lax.div(j, 2), lax.rem(j, 2)])

    def get_down(k):
        part = pl.ds(*down_rows[k])
        return load(9 + k, f_down.at[:, :, :, :, part], wa.at[:, :, :, :, part])

    ag.tick(15)
    maker.flush()
    rs.stage(0, 0)
    ag.tick(16)
    ag.tick(17)
    rs.stage(1, 0)
    for k in range(len(down_rows)):
        ag.stage(10 + k, 4)
        get_down(k).start()
    for k in range(len(down_rows)):
        get_down(k).wait()
    rs.stage(2, 0)
    for k in range(2):
        cols = pl.ds(k * TILE, TILE)
        w = wa[:, :, :, :, :, cols].reshape(ff, TILE)
        go[:, cols] = (x1[:, cols] + dot_nn(flat(a, slice(None)), w)).astype(BF)

    outs = []
    for q in quarters:
        outs.append(
            (
                pltpu.make_async_copy(go.at[q], fo.at[q], io_sem.at[len(outs)]),
                remote(go.at[q], fo.at[q], io_sem.at[len(outs)], io_recv.at[len(outs)], far),
            )
        )

    def either(pair, act_on):
        @pl.when(straight)
        def _():
            act_on(pair[0])

        @pl.when(jnp.logical_not(straight))
        def _():
            act_on(pair[1])

    def begin(pair):
        either(pair, lambda copy: copy.start())

    def end(pair):
        either(pair, lambda copy: copy.wait())

    begin(outs[0])
    def act(j, cols):
        w = wa[lax.div(j, 2), lax.rem(j, 2)].reshape(TILE, d)
        v = dot_nt(cot[...], w) * flat(gp, cols).astype(F32)
        gp[:, :, :, :, cols] = v.astype(BF).reshape(a.shape[:-1] + (TILE,))

    rs.tick(1)
    rs.stage(3, 0)
    tiles(8, TILE, act)
    begin(outs[1])
    for i, b in enumerate((3, 0, 1, 2)):
        load_block(14 + i, b).start()
    ht[...] = h2[...].T
    for i in range(2):
        gh[:, pl.ds(i * TILE, TILE)] = dot_nt(flat(gp, slice(None)), wb[2 * i : 2 * i + 2].reshape(TILE, ff))
        if i == 0:
            rs.tick(2)
    begin(outs[2])
    acc[...] = jnp.zeros_like(acc)
    step = 32

    def collect(row, v):
        part = v.reshape(step // 8, 8, d)
        acc[row] = acc[row] + functools.reduce(jnp.add, [part[i] for i in range(step // 8)])

    def back_two(j, part):
        nrm, scale = normalise(x1[part, :])
        g = gh[part, :]
        collect(1, g * nrm)
        collect(3, g)
        total = cot[part, :].astype(F32) + norm_back(g, nrm, scale, par[1:2, :])
        x1[part, :] = total
        gz[part, :] = total.astype(BF)

    tiles(rows // step, step, back_two)

    def row_half(j):
        return ht[pl.ds(pl.multiple_of(lax.rem(j, 2) * TILE, TILE), TILE), :]

    def wide(j):
        return pl.ds(pl.multiple_of(lax.div(j, 2) * WIDE, WIDE), WIDE)

    def up_product(j):
        return dot_nn(row_half(j), flat(gp, wide(j)))

    def target(ref, first):
        def of(j, i):
            cols = pl.ds(pl.multiple_of(first + lax.div(j, 2) * WIDE, WIDE), WIDE)
            return ref.at[2 * lax.rem(j, 2) + i // 2, i % 2, :, :, cols]

        return of

    rs.tick(3)
    begin(outs[3])
    maker.run(
        2 * ups, up_product, row_blocks, target(a, 0), {2: rs_begin(4), 3: rs_tick(4), 4: rs_begin(5), 6: rs_begin(6)}
    )
    maker.flush()
    rs.stage(7, 0)
    for pair in outs:
        end(pair)
    load_block(14, 3).wait()
    for i in range(2):
        go[:, pl.ds(i * TILE, TILE)] = dot_nt(gz[...], block(3, pl.ds(2 * i, 2))).astype(BF)
    pick = (
        lax.broadcasted_iota(jnp.int32, (H, d), 1) // HD == lax.broadcasted_iota(jnp.int32, (H, d), 0)
    ).astype(BF)
    for i in range(4):
        part = pl.ds(i * quarter, quarter)
        prod = go[part, :].astype(F32) * att[part, :].astype(F32)
        high = prod.astype(BF)
        low = (prod - high.astype(F32)).astype(BF)
        deltat[:, part] = dot_nt(pick, high) + dot_nt(pick, low)
    low_cols, high_cols = pl.ds(0, SHARED * PAIR), pl.ds(SHARED * PAIR, d - SHARED * PAIR)
    high_cols2 = pl.ds(d + SHARED * PAIR, d - SHARED * PAIR)
    low_cols2 = pl.ds(d, SHARED * PAIR)

    lends = [
        between(9, qkv.at[:, high_cols], cross.at[:, high_cols]),
        between(15, go.at[:, high_cols], cross.at[:, high_cols2]),
        between(16, lset, far_lse),
        between(10, deltat, far_delta),
    ]
    gives = [
        between(11, cross.at[:, low_cols], cross.at[:, low_cols]),
        between(12, cross.at[:, low_cols2], cross.at[:, low_cols2]),
    ]
    returns = between(13, cross.at[:, high_cols], cross.at[:, high_cols])

    @pl.when(c == 1)
    def _():
        for copy in lends:
            copy.start()

    rs.tick(5)
    ht[...] = att[...].T
    maker.run(2, lambda j: dot_nn(row_half(j), gz[...]), row_blocks, target(gp, 3 * d))
    fill_bias(bias, pre[0:1, 0:1], c, True)

    @pl.when(c == 0)
    def _():
        for copy in lends:
            copy.wait_recv()

    @pl.when(c == 1)
    def _():
        for copy in lends:
            copy.wait_send()

    def give_back():
        @pl.when(c == 1)
        def _():
            for copy in gives:
                copy.start()

    def return_queries():
        @pl.when(c == 0)
        def _():
            returns.start()

    def flush_tick():
        maker.flush()
        rs.stage(8, 0)
        rs.tick(6)

    hooks = {0: flush_tick, 2: return_queries, 3: rs_tick(7), 4: give_back, 5: rs_tick(8), 7: rs_tick(9)}
    attend_backward(c, qkv, cross, bias, lset, deltat, far_lse, far_delta, go, narrow, narrow2, gh, hooks)
    ht[...] = h1[...].T

    @pl.when(c == 1)
    def _():
        for copy in gives:
            copy.wait_send()
        returns.wait_recv()

        def add(j, part):
            qkv[part, high_cols] = (qkv[part, high_cols].astype(F32) + cross[part, high_cols].astype(F32)).astype(BF)

        tiles(rows // step, step, add)

    @pl.when(c == 0)
    def _():
        returns.wait_send()
        for copy in gives:
            copy.wait_recv()

        def add(j, part):
            for base in (0, d):
                to, src = pl.ds(d + base, SHARED * PAIR), pl.ds(base, SHARED * PAIR)
                qkv[part, to] = (qkv[part, to].astype(F32) + cross[part, src].astype(F32)).astype(BF)

        tiles(rows // step, step, add)

    def mixed_cols(j):
        return pl.ds(pl.multiple_of(lax.rem(lax.div(j, 2) + 1, 3) * d, d), d)

    def mixed_target(j, i):
        return gp.at[2 * lax.rem(j, 2) + i // 2, i % 2, :, :, mixed_cols(j)]

    maker.run(
        6, lambda j: dot_nn(row_half(j), qkv[:, mixed_cols(j)]), row_blocks, mixed_target, {2: rs_begin(9), 4: rs_begin(10)}
    )
    maker.flush()
    rs.stage(11, 0)
    rs.stage(12, 0)
    for i, b in enumerate((0, 1, 2)):
        load_block(15 + i, b).wait()
    for i in range(2):
        total = None
        for b in range(3):
            part = dot_nt(qkv[:, pl.ds(b * d, d)], block(b, pl.ds(2 * i, 2)))
            total = part if total is None else total + part
        gh[:, pl.ds(i * TILE, TILE)] = total
        if i == 0:
            rs.tick(10)

    def back_one(j, part):
        nrm, scale = normalise(x[part, :].astype(F32))
        g = gh[part, :]
        collect(0, g * nrm)
        collect(2, g)
        total = x1[part, :] + norm_back(g, nrm, scale, par[0:1, :])
        gh[part, :] = total
        gz[part, :] = total.astype(BF)

    tiles(rows // step, step, back_one)
    backs = []
    for i, q in enumerate(quarters):
        backs.append(
            (
                pltpu.make_async_copy(gh.at[q], gi.at[q], io_sem.at[4 + i]),
                remote(gz.at[q], gl.at[q], io_sem.at[4 + i], io_recv.at[4 + i], far),
            )
        )
    begin(backs[0])
    for i in range(4):
        par[i : i + 1, :] = jnp.sum(acc[i], 0, keepdims=True)
    for t in range(d // PAIR):
        row = par[:, pl.ds(t * PAIR, PAIR)].astype(BF)
        for k in range(2):
            spar[t // 2, t % 2, k] = row
            ptheirs[t // 2, t % 2, k] = row
    pars = remote(ptheirs, pland, io_sem.at[8], io_recv.at[8], core)
    pars.start()
    rs.tick(11)
    begin(backs[1])
    rs.tick(12)
    pars.wait_recv()
    add_blocks(spar, [pland])
    rs.stage(n, 0)
    rs.tick(13)
    begin(backs[2])
    rs.tick(14)
    begin(backs[3])
    rs.tick(15)
    rs.tick(16)
    for pair in backs:
        end(pair)
    pars.wait_send()
    for i in range(len(chunks)):
        ag.finish(i)
    for i in range(n + 1):
        rs.finish(i)
    maker.finish()


def layer(nz, frames_in, cot, pre, w_qkv, w_out, w_up, w_down, tile):
    rows, d = frames_in.shape
    ff = w_up.shape[1]
    S = jax.ShapeDtypeStruct
    V = pltpu.VMEM
    REG = pltpu.SemaphoreType.REGULAR
    hbm, vm = pl.BlockSpec(memory_space=pl.ANY), pl.BlockSpec(memory_space=V)
    shards = (w_qkv, w_out, w_up, w_down, tile)
    parts = (nz, 2, 2, BLOCK)
    full = (nz, 2, 2, 2)
    return pl.pallas_call(
        functools.partial(layer_kernel, nz),
        out_shape=[S((rows, d), BF), S((rows, d), F32), S((rows, d), BF)]
        + [S(full + w.shape, BF) for w in shards]
        + [S(w.shape, F32) for w in shards],
        in_specs=[hbm] * 8,
        out_specs=[hbm] * 8 + [vm] * 5,
        scratch_shapes=[
            V((rows, d), BF), V((rows, d), BF), V((8, PAIR), jnp.int32), V((rows, d), BF), V((rows, 3 * d), BF),
            V((rows, 2 * d), BF), V((rows, d), BF), V((rows, d), F32), V((rows, d), BF),
            V(parts + (ff,), BF), V(parts + (ff,), BF),
            V(full + w_down.shape, BF), V(full + w_up.shape, BF),
            V((rows, d), F32), V((rows, d), BF), V((rows, d), BF), V((rows, rows), F32), V((rows, PAIR), F32), V((rows, PAIR), F32),
            V((H, rows), F32), V((H, rows), F32), V((H, rows), F32), V((H, rows), F32), V((4, 8, d), F32), V((16, d), F32), V(full + (16, PAIR), BF),
            V((d, rows), BF), V((2, 4, 2, 2, BLOCK, WIDE), BF), V((2, 4, 2, BLOCK, WIDE), BF),
            V((4,) + parts + (d,), BF), V((nz, 2, 2, 16, PAIR), BF), V((nz, 2, 2, 16, PAIR), BF), V((nz, 2, 2, 16, PAIR), BF),
            V((RING, nz, 2, BLOCK, WIDE), BF), V((RING, 7, BLOCK, WIDE), BF), V((nz, 2, 16, PAIR), BF), V((7, 16, PAIR), BF),
        ]
        + Gather.sem_shapes(15)
        + Scatter.sem_shapes(14)
        + [DMA((2,)), DMA((2,)), REG((2,)), DMA((18,)), DMA((17, 3)), DMA((9,)), DMA((9,))],
        compiler_params=pltpu.CompilerParams(collective_id=0, has_side_effects=True, vmem_limit_bytes=63 * 2**20),
    )(frames_in, cot, pre, *shards)


def settle_kernel(fo, gi, gl, g_qkv, g_out, g_up, g_down, g_par, fo_, gi_, qkv_, out_, up_, down_, gains_, shifts_, narrow, wide, *rest):
    straight = lax.rem(lax.axis_index("dp"), 2) == lax.axis_index("fsdp")
    stops, sems = rest[:5], rest[5]
    pairs = ((fo, fo_), (g_qkv, qkv_), (g_out, out_), (g_up, up_), (g_down, down_))
    ins = [pltpu.make_async_copy(src, stop, sems.at[0, i]) for i, ((src, _), stop) in enumerate(zip(pairs, stops))]
    outs = [pltpu.make_async_copy(stop, dst, sems.at[1, i]) for i, ((_, dst), stop) in enumerate(zip(pairs, stops))]
    rows = gi.shape[0] // 4
    parts = [pl.ds(i * rows, rows) for i in range(4)]
    own = [pltpu.make_async_copy(gi.at[p], wide.at[p], sems.at[2, i]) for i, p in enumerate(parts)]
    came = [pltpu.make_async_copy(gl.at[p], narrow.at[p], sems.at[2, i]) for i, p in enumerate(parts)]
    puts = [pltpu.make_async_copy(wide.at[p], gi_.at[p], sems.at[3, i]) for i, p in enumerate(parts)]

    @pl.when(straight)
    def _():
        for get in own:
            get.start()

    @pl.when(jnp.logical_not(straight))
    def _():
        for get in came:
            get.start()

    for copy in ins:
        copy.start()
    width = gains_.shape[1]
    mine = lax.rem(lax.axis_index("dp") * 2 + lax.axis_index("fsdp"), PAIR // width)
    small = g_par[:, pl.ds(0, width)]
    for i in range(1, PAIR // width):
        small = jnp.where(mine == i, g_par[:, pl.ds(i * width, width)], small)
    gains_[...] = small[0:2]
    shifts_[...] = small[2:4]

    @pl.when(straight)
    def _():
        for get, put in zip(own, puts):
            get.wait()
            put.start()

    @pl.when(jnp.logical_not(straight))
    def _():
        for get, put, p in zip(came, puts, parts):
            get.wait()
            wide[p, :] = narrow[p, :].astype(F32)
            put.start()

    for get, put in zip(ins, outs):
        get.wait()
        put.start()
    for put in puts + outs:
        put.wait()


def settle(width, fo, gi, gl, *grads):
    S = jax.ShapeDtypeStruct
    V = pltpu.VMEM
    hbm, vm = pl.BlockSpec(memory_space=pl.ANY), pl.BlockSpec(memory_space=V)
    kept = (fo, gi) + grads[:4]
    return pl.pallas_call(
        settle_kernel,
        out_shape=[S(v.shape, v.dtype) for v in kept] + [S((2, width), F32)] * 2,
        in_specs=[hbm] * 7 + [vm],
        out_specs=[hbm] * 6 + [vm] * 2,
        scratch_shapes=[V(gl.shape, BF), V(gi.shape, F32)] + [V(v.shape, v.dtype) for v in (fo,) + grads[:4]] + [DMA((4, 5))],
        compiler_params=pltpu.CompilerParams(vmem_limit_bytes=VMEM_LIMIT),
    )(fo, gi, gl, *grads)


def norm_rows(values, gain, shift):
    center = values - jnp.mean(values, -1, keepdims=True)
    spread = jnp.mean(center * center, -1, keepdims=True)
    return center * lax.rsqrt(spread + EPS) * gain + shift


def collect(w_qkv, w_out, w_up, w_down, gains, shifts):
    return (
        lax.all_gather(w_qkv, ("dp", "fsdp"), axis=0, tiled=True),
        lax.all_gather(w_out, ("dp", "fsdp"), axis=0, tiled=True),
        lax.all_gather(w_up, ("dp", "fsdp"), axis=0, tiled=True),
        lax.all_gather(w_down, ("dp", "fsdp"), axis=0, tiled=True),
        lax.all_gather(gains, ("dp", "fsdp"), axis=1, tiled=True),
        lax.all_gather(shifts, ("dp", "fsdp"), axis=1, tiled=True),
    )


def split_heads(matrix):
    return matrix.reshape(matrix.shape[0], H, HD).transpose(1, 0, 2)


def join_heads(stacked):
    return stacked.transpose(1, 0, 2).reshape(stacked.shape[1], H * HD)


def masked_scores(query_one, key_one, allowed):
    scores = jnp.dot(query_one, key_one.T, preferred_element_type=jnp.float32) * 0.125
    return jnp.where(allowed, scores, -1e30)


def forward(inputs, weights, allowed):
    w_qkv, w_out, w_up, w_down, gains, shifts = weights
    width = inputs.shape[1]
    gain_rows = gains.astype(jnp.float32)
    shift_rows = shifts.astype(jnp.float32)
    normed = norm_rows(inputs, gain_rows[0], shift_rows[0]).astype(jnp.bfloat16)
    mixed = jnp.dot(normed, w_qkv, preferred_element_type=jnp.float32).astype(jnp.bfloat16)
    queries = mixed[:, :width]
    keys_all, values_all = (
        lax.all_gather(mixed[:, width : 2 * width], "fsdp", axis=0, tiled=True),
        lax.all_gather(mixed[:, 2 * width :], "fsdp", axis=0, tiled=True),
    )
    query_heads = split_heads(queries)
    key_heads = split_heads(keys_all)
    value_heads = split_heads(values_all)

    def single(pieces):
        scores = masked_scores(pieces[0], pieces[1], allowed)
        peak_row = jnp.max(scores, -1, keepdims=True)
        log_total = peak_row + jnp.log(jnp.sum(jnp.exp(scores - peak_row), -1, keepdims=True))
        chance = jnp.exp(scores - log_total).astype(jnp.bfloat16)
        return (jnp.dot(chance, pieces[2], preferred_element_type=jnp.float32), log_total[:, 0])

    outputs, totals = lax.map(single, (query_heads, key_heads, value_heads))
    attended = join_heads(outputs).astype(jnp.bfloat16)
    middle = inputs + jnp.dot(attended, w_out, preferred_element_type=jnp.float32)
    normed_two = norm_rows(middle, gain_rows[1], shift_rows[1]).astype(jnp.bfloat16)
    hidden = jnp.dot(normed_two, w_up, preferred_element_type=jnp.float32)
    active = jax.nn.gelu(hidden, approximate=False).astype(jnp.bfloat16)
    result = middle + jnp.dot(active, w_down, preferred_element_type=jnp.float32)
    saved = (
        normed,
        query_heads,
        key_heads,
        value_heads,
        totals,
        attended,
        middle,
        normed_two,
        hidden,
        active,
    )
    return (result, saved)


def on_device(frames_in, prefix_len, w_qkv, w_out, w_up, w_down, gains, shifts, cotangent):
    inputs = frames_in[0].astype(jnp.float32)
    rows_here = inputs.shape[0]
    frames_all = rows_here * lax.axis_size("fsdp")
    first_row = lax.axis_index("fsdp") * rows_here
    places = first_row + jnp.arange(rows_here, dtype=jnp.int32)
    columns = jnp.arange(frames_all, dtype=jnp.int32)
    allowed = (columns[None, :] <= places[:, None]) | (columns[None, :] < prefix_len[0])
    weights = collect(w_qkv, w_out, w_up, w_down, gains, shifts)
    result, saved = forward(inputs, weights, allowed)
    weights = collect(w_qkv, w_out, w_up, w_down, gains, shifts)
    saved = forward(inputs, weights, allowed)[1]
    full_qkv, full_out, full_up, full_down, full_gains, full_shifts = weights
    (
        normed,
        query_heads,
        key_heads,
        value_heads,
        totals,
        attended,
        middle,
        normed_two,
        hidden,
        active,
    ) = saved
    gain_rows = full_gains.astype(jnp.float32)
    shift_rows = full_shifts.astype(jnp.float32)
    grad_top = cotangent[0].astype(jnp.float32)
    grad_branch = grad_top.astype(jnp.bfloat16)
    part_down = jnp.dot(active.T, grad_branch, preferred_element_type=jnp.float32)
    grad_active = jnp.dot(grad_branch, full_down.T, preferred_element_type=jnp.float32)
    gelu_pull = jax.vjp(functools.partial(jax.nn.gelu, approximate=False), hidden)[1]
    grad_hidden = gelu_pull(grad_active)[0].astype(jnp.bfloat16)
    part_up = jnp.dot(normed_two.T, grad_hidden, preferred_element_type=jnp.float32)
    grad_normed_two = jnp.dot(grad_hidden, full_up.T, preferred_element_type=jnp.float32)
    norm_pull_two = jax.vjp(norm_rows, middle, gain_rows[1], shift_rows[1])[1]
    back_middle, grad_gain_two, grad_shift_two = norm_pull_two(grad_normed_two)
    grad_middle = grad_top + back_middle
    grad_attn_out = grad_middle.astype(jnp.bfloat16)
    part_out = jnp.dot(attended.T, grad_attn_out, preferred_element_type=jnp.float32)
    grad_attended = jnp.dot(grad_attn_out, full_out.T, preferred_element_type=jnp.float32).astype(
        jnp.bfloat16
    )
    grad_att_heads = split_heads(grad_attended)

    def single_back(pieces):
        query_one, key_one, value_one, grad_one, log_total = pieces
        scores = masked_scores(query_one, key_one, allowed)
        chance = jnp.exp(scores - log_total[:, None])
        grad_chance = jnp.dot(grad_one, value_one.T, preferred_element_type=jnp.float32)
        inner = jnp.sum(chance * grad_chance, -1, keepdims=True)
        grad_scores = (chance * (grad_chance - inner)).astype(jnp.bfloat16)
        grad_query = jnp.dot(grad_scores, key_one, preferred_element_type=jnp.float32) * 0.125
        grad_key = (
            jnp.einsum("qk,qd->kd", grad_scores, query_one, preferred_element_type=jnp.float32)
            * 0.125
        )
        grad_value = jnp.einsum(
            "qk,qd->kd", chance.astype(jnp.bfloat16), grad_one, preferred_element_type=jnp.float32
        )
        return (grad_query, grad_key, grad_value)

    grad_q_heads, grad_k_heads, grad_v_heads = lax.map(
        single_back, (query_heads, key_heads, value_heads, grad_att_heads, totals)
    )
    grad_keys, grad_values = (
        lax.psum_scatter(
            join_heads(grad_k_heads).astype(jnp.bfloat16), "fsdp", scatter_dimension=0, tiled=True
        ).astype(jnp.float32),
        lax.psum_scatter(
            join_heads(grad_v_heads).astype(jnp.bfloat16), "fsdp", scatter_dimension=0, tiled=True
        ).astype(jnp.float32),
    )
    grad_mixed = jnp.concatenate([join_heads(grad_q_heads), grad_keys, grad_values], 1).astype(
        jnp.bfloat16
    )
    part_qkv = jnp.dot(normed.T, grad_mixed, preferred_element_type=jnp.float32)
    grad_normed = jnp.dot(grad_mixed, full_qkv.T, preferred_element_type=jnp.float32)
    norm_pull_one = jax.vjp(norm_rows, inputs, gain_rows[0], shift_rows[0])[1]
    back_inputs, grad_gain_one, grad_shift_one = norm_pull_one(grad_normed)
    grad_inputs = grad_middle + back_inputs
    part_gains = jnp.stack([grad_gain_one, grad_gain_two])
    part_shifts = jnp.stack([grad_shift_one, grad_shift_two])
    owned = (
        lax.psum_scatter(part_qkv, ("dp", "fsdp"), scatter_dimension=0, tiled=True),
        lax.psum_scatter(part_out, ("dp", "fsdp"), scatter_dimension=0, tiled=True),
        lax.psum_scatter(part_up, ("dp", "fsdp"), scatter_dimension=0, tiled=True),
        lax.psum_scatter(part_down, ("dp", "fsdp"), scatter_dimension=0, tiled=True),
        lax.psum_scatter(part_gains, ("dp", "fsdp"), scatter_dimension=1, tiled=True),
        lax.psum_scatter(part_shifts, ("dp", "fsdp"), scatter_dimension=1, tiled=True),
    )
    return (
        result.astype(jnp.bfloat16)[None],
        grad_inputs[None],
        owned[0],
        owned[1],
        owned[2],
        owned[3],
        owned[4],
        owned[5],
    )


def fast_device(ndp, frames_in, prefix_len, w_qkv, w_out, w_up, w_down, gains, shifts, cotangent):
    here = lax.axis_index("dp") * 2 + lax.axis_index("fsdp")
    width = gains.shape[1]
    per = PAIR // width
    rows = jnp.concatenate([gains, shifts, jnp.zeros((12, width), BF)], 0)
    tile = jnp.where(lax.broadcasted_iota(jnp.int32, (16, per, width), 1) == here % per, rows[:, None], 0.0)
    tile = tile.astype(BF).reshape(16, PAIR)
    pre = jnp.broadcast_to(prefix_len[None], (8, PAIR))
    result = layer(ndp // 4, frames_in[0], cotangent[0], pre, w_qkv, w_out, w_up, w_down, tile)
    frames_out, grad_in, *owned = settle(width, *result[:3], *result[8:])
    return (frames_out[None], grad_in[None]) + tuple(owned)


def solution(mesh):
    ndp, nf = mesh.shape["dp"], mesh.shape["fsdp"]
    both = P(("dp", "fsdp"), None)
    lanes = P(None, ("dp", "fsdp"))
    block = P("dp", "fsdp", None)
    body = functools.partial(fast_device, ndp) if (nf == 2 and ndp == 16) else on_device
    return jax.shard_map(
        body,
        mesh=mesh,
        in_specs=(block, P("dp"), both, both, both, both, lanes, lanes, block),
        out_specs=(block, block, both, both, both, both, lanes, lanes),
        check_vma=False,
    )
```

profile of v0, /device:TPU:0, one launch (start us, length us, event | category | flops | bytes accessed | tf_op | source)
XLA Modules:
  0.0 295.4 jit_solution(5694586493907989452)
XLA Ops:
  1.3 0.1 iota.11
  1.4 0.1 iota.12
  1.5 0.1 pad.2.clone
  1.5 0.7 maximum_maximum_fusion
  2.3 0.6 broadcast_in_dim.33.refs_2_
  2.9 0.1 broadcast_in_dim.36
  3.0 0.6 broadcast_select_fusion.refs_7_
  3.6 286.2 %shard_map.152 = (bf16[512,1024]{1,0:T(8,128)(2,1)}, f32[512,1024]{1,0:T(8,128)}, bf16[512,1024]{1,0:T(8,128)(2,1)}, bf16[4,2,2,2,32,3072]{5,4,3,2,1,0:T(8,128)(...) custom-call(bf16[512,1024]{1,0:T(8,128)(2,1)} %bitcast.6, ...), custom_call_target="tpu_custom_call" | custom-call | tf_op jit(solution)/shard_map/pallas_call | solution.py:1095
  289.8 5.5 %shard_map.153 = (bf16[512,1024]{1,0:T(8,128)(2,1)}, f32[512,1024]{1,0:T(8,128)}, f32[32,3072]{1,0:T(8,128)}, f32[32,1024]{1,0:T(8,128)}, f32[32,4096]{1,0:T(8,1...) custom-call(bf16[512,1024]{1,0:T(8,128)(2,1)} %get-tuple-element.24.fo, ...), custom_call_target="tpu_custom_call" | custom-call | tf_op jit(solution)/shard_map/pallas_call | solution.py:1177
  (3 shorter events, 0.0 us)
where the time goes:
time: 299 us; the launch traced here: 295 us
  Pallas kernels  292 us (98%)
    pallas_call x1, Pallas kernels, layer(): pl.pallas_call(functools.partial(layer_kernel, nz), out_shape=[S((rows, d...  286 us

commit v1 on v0

--- a/solution.py
+++ b/solution.py
@@ -183,8 +183,8 @@
                     for copy in self.copies(i)[core][s]:
                         copy.start()
 
-    def tick(self, t):
-        for s in range(4):
+    def tick(self, t, stages=(0, 1, 2, 3)):
+        for s in stages:
             if 0 <= t - s < len(self.chunks):
                 self.stage(t - s, s)
 
@@ -744,7 +744,7 @@
 
     swap_start(4)
     narrow[...] = jnp.zeros_like(narrow)
-    attend_forward(c, qkv, cross, bias, att, narrow, {1: ag_tick(8), 6: ag_tick(9)})
+    attend_forward(c, qkv, cross, bias, att, narrow, {0: ag_tick(8), 5: ag_tick(9)})
     ag.stage(5, 4)
     get_out = load_block(4, 3)
     get_out.start()
@@ -803,9 +803,13 @@
         up(cols)
         for k in range(ups):
 
+            @pl.when(j == 2 * k)
+            def _():
+                ag.tick(11 + k, (0, 1))
+
             @pl.when(j == 2 * k + 1)
             def _():
-                ag.tick(11 + k)
+                ag.tick(11 + k, (2, 3))
 
         return dot_tn(flat(a, cols), cot[...])
 
@@ -817,17 +821,16 @@
 
     ag.tick(15)
     maker.flush()
-    rs.stage(0, 0)
     ag.tick(16)
     ag.tick(17)
-    rs.stage(1, 0)
+    rs.stage(0, 0)
     for k in range(len(down_rows)):
         ag.stage(10 + k, 4)
         get_down(k).start()
     for k in range(len(down_rows)):
         get_down(k).wait()
-    rs.stage(2, 0)
     for k in range(2):
+        rs.stage(1 + k, 0)
         cols = pl.ds(k * TILE, TILE)
         w = wa[:, :, :, :, :, cols].reshape(ff, TILE)
         go[:, cols] = (x1[:, cols] + dot_nn(flat(a, slice(None)), w)).astype(BF)
@@ -981,7 +984,7 @@
         rs.stage(8, 0)
         rs.tick(6)
 
-    hooks = {0: flush_tick, 2: return_queries, 3: rs_tick(7), 4: give_back, 5: rs_tick(8), 7: rs_tick(9)}
+    hooks = {0: flush_tick, 2: return_queries, 3: rs_tick(7), 4: give_back, 6: rs_tick(8)}
     attend_backward(c, qkv, cross, bias, lset, deltat, far_lse, far_delta, go, narrow, narrow2, gh, hooks)
     ht[...] = h1[...].T
 
@@ -1016,7 +1019,7 @@
         return gp.at[2 * lax.rem(j, 2) + i // 2, i % 2, :, :, mixed_cols(j)]
 
     maker.run(
-        6, lambda j: dot_nn(row_half(j), qkv[:, mixed_cols(j)]), row_blocks, mixed_target, {2: rs_begin(9), 4: rs_begin(10)}
+        6, lambda j: dot_nn(row_half(j), qkv[:, mixed_cols(j)]), row_blocks, mixed_target, {1: rs_tick(9), 2: rs_begin(9), 4: rs_begin(10)}
     )
     maker.flush()
     rs.stage(11, 0)
@@ -1061,17 +1064,18 @@
     pars = remote(ptheirs, pland, io_sem.at[8], io_recv.at[8], core)
     pars.start()
     rs.tick(11)
-    begin(backs[1])
-    rs.tick(12)
     pars.wait_recv()
     add_blocks(spar, [pland])
     rs.stage(n, 0)
-    rs.tick(13)
+    begin(backs[1])
+    for i, st in ((11, 1), (12, 1), (10, 2), (9, 3)):
+        rs.stage(i, st)
     begin(backs[2])
-    rs.tick(14)
+    for i, st in ((n, 1), (11, 2), (12, 2)):
+        rs.stage(i, st)
     begin(backs[3])
-    rs.tick(15)
-    rs.tick(16)
+    for i, st in ((10, 3), (n, 2), (11, 3), (12, 3), (n, 3)):
+        rs.stage(i, st)
     for pair in backs:
         end(pair)
     pars.wait_send()

time: 299 us -> 284 us (0.950)
  Pallas kernels: 292 us -> 277 us
    pallas_call x1, Pallas kernels: 286 us -> 272 us  [layer(): pl.pallas_call(functools.partial(layer_kernel, nz), out_shape=[S((rows, d...]
where the time goes in v1:
time: 284 us; the launch traced here: 281 us
  Pallas kernels  277 us (98%)
    pallas_call x1, Pallas kernels, layer(): pl.pallas_call(functools.partial(layer_kernel, nz), out_shape=[S((rows, d...  272 us

profile of v1, /device:TPU:0, one launch (start us, length us, event | category | flops | bytes accessed | tf_op | source)
XLA Modules:
  0.0 281.1 jit_solution(7607589804444391897)
XLA Ops:
  1.3 0.1 iota.11
  1.4 0.1 iota.12
  1.5 0.1 pad.2.clone
  1.5 0.7 maximum_maximum_fusion
  2.3 0.6 broadcast_in_dim.33.refs_2_
  2.9 0.1 broadcast_in_dim.36
  3.0 0.6 broadcast_select_fusion.refs_7_
  3.6 271.8 %shard_map.152 = (bf16[512,1024]{1,0:T(8,128)(2,1)}, f32[512,1024]{1,0:T(8,128)}, bf16[512,1024]{1,0:T(8,128)(2,1)}, bf16[4,2,2,2,32,3072]{5,4,3,2,1,0:T(8,128)(...) custom-call(bf16[512,1024]{1,0:T(8,128)(2,1)} %bitcast.6, ...), custom_call_target="tpu_custom_call" | custom-call | tf_op jit(solution)/shard_map/pallas_call | solution.py:1099
  275.4 5.5 %shard_map.153 = (bf16[512,1024]{1,0:T(8,128)(2,1)}, f32[512,1024]{1,0:T(8,128)}, f32[32,3072]{1,0:T(8,128)}, f32[32,1024]{1,0:T(8,128)}, f32[32,4096]{1,0:T(8,1...) custom-call(bf16[512,1024]{1,0:T(8,128)(2,1)} %get-tuple-element.24.fo, ...), custom_call_target="tpu_custom_call" | custom-call | tf_op jit(solution)/shard_map/pallas_call | solution.py:1181
  (3 shorter events, 0.0 us)

commit v2 on v1

--- a/solution.py
+++ b/solution.py
@@ -610,8 +610,8 @@
     chunks += [(0, 0, BLOCK, d + h * TILE, TILE) for h in range(2)] + [(0, 0, BLOCK, b * d, d) for b in (2, 0)]
     chunks += [(1, 0, BLOCK, 0, d)]
     chunks += [(2, 0, BLOCK, k * WIDE, WIDE) for k in range(ff // WIDE)]
-    down_rows = [(0, BLOCK), (BLOCK, BLOCK), (2 * BLOCK, BLOCK), (3 * BLOCK, BLOCK // 2), (7 * BLOCK // 2, BLOCK // 2)]
-    chunks += [(3, r0, r, 0, d) for r0, r in down_rows]
+    down_cols = [(0, 256), (256, 256), (512, 256), (768, 128), (896, 128)]
+    chunks += [(3, 0, 4 * BLOCK, c0, w) for c0, w in down_cols]
     ag = Gather(nz, place, (s_qkv, s_out, s_up, s_down, s_par), (f_qkv, f_out, f_up, f_down, f_par), chunks, (ag_send, ag_recv, ag_own))
 
     ups, downs = ff // WIDE, 4
@@ -816,25 +816,33 @@
     maker.run(2 * ups, down_product, deep_blocks, lambda j, i: sdown.at[i, lax.div(j, 2), lax.rem(j, 2)])
 
     def get_down(k):
-        part = pl.ds(*down_rows[k])
-        return load(9 + k, f_down.at[:, :, :, :, part], wa.at[:, :, :, :, part])
+        part = pl.ds(*down_cols[k])
+        return load(9 + k, f_down.at[:, :, :, :, :, part], wa.at[:, :, :, :, :, part])
+
+    def down(k):
+        cols = pl.ds(k * TILE, TILE)
+        w = wa[:, :, :, :, :, cols].reshape(ff, TILE)
+        go[:, cols] = (x1[:, cols] + dot_nn(flat(a, slice(None)), w)).astype(BF)
 
     ag.tick(15)
     maker.flush()
+    for k in range(2):
+        ag.stage(10 + k, 4)
+        get_down(k).start()
     ag.tick(16)
     ag.tick(17)
     rs.stage(0, 0)
-    for k in range(len(down_rows)):
+    for k in range(2):
+        get_down(k).wait()
+    down(0)
+    for k in range(2, len(down_cols)):
         ag.stage(10 + k, 4)
         get_down(k).start()
-    for k in range(len(down_rows)):
+    for k in range(2, len(down_cols)):
         get_down(k).wait()
-    for k in range(2):
-        rs.stage(1 + k, 0)
-        cols = pl.ds(k * TILE, TILE)
-        w = wa[:, :, :, :, :, cols].reshape(ff, TILE)
-        go[:, cols] = (x1[:, cols] + dot_nn(flat(a, slice(None)), w)).astype(BF)
-
+    rs.stage(1, 0)
+    down(1)
+    rs.stage(2, 0)
     outs = []
     for q in quarters:
         outs.append(
@@ -865,9 +873,8 @@
         v = dot_nt(cot[...], w) * flat(gp, cols).astype(F32)
         gp[:, :, :, :, cols] = v.astype(BF).reshape(a.shape[:-1] + (TILE,))
 
-    rs.tick(1)
     rs.stage(3, 0)
-    tiles(8, TILE, act)
+    tiles(8, TILE, act, {5: rs_tick(1)})
     begin(outs[1])
     for i, b in enumerate((3, 0, 1, 2)):
         load_block(14 + i, b).start()
@@ -1024,6 +1031,7 @@
     maker.flush()
     rs.stage(11, 0)
     rs.stage(12, 0)
+    rs.tick(10)
     for i, b in enumerate((0, 1, 2)):
         load_block(15 + i, b).wait()
     for i in range(2):
@@ -1032,8 +1040,8 @@
             part = dot_nt(qkv[:, pl.ds(b * d, d)], block(b, pl.ds(2 * i, 2)))
             total = part if total is None else total + part
         gh[:, pl.ds(i * TILE, TILE)] = total
-        if i == 0:
-            rs.tick(10)
+        if i == 1:
+            rs.tick(11)
 
     def back_one(j, part):
         nrm, scale = normalise(x[part, :].astype(F32))
@@ -1063,12 +1071,12 @@
             ptheirs[t // 2, t % 2, k] = row
     pars = remote(ptheirs, pland, io_sem.at[8], io_recv.at[8], core)
     pars.start()
-    rs.tick(11)
+    rs.stage(11, 1)
     pars.wait_recv()
     add_blocks(spar, [pland])
     rs.stage(n, 0)
     begin(backs[1])
-    for i, st in ((11, 1), (12, 1), (10, 2), (9, 3)):
+    for i, st in ((12, 1), (10, 2), (9, 3)):
         rs.stage(i, st)
     begin(backs[2])
     for i, st in ((n, 1), (11, 2), (12, 2)):

time: 284 us -> 284 us (level)
  no operation moved by 1% of the time
where the time goes in v2:
time: 284 us; the launch traced here: 281 us
  Pallas kernels  278 us (98%)
    pallas_call x1, Pallas kernels, layer(): pl.pallas_call(functools.partial(layer_kernel, nz), out_shape=[S((rows, d...  272 us

profile of v2, /device:TPU:0, one launch (start us, length us, event | category | flops | bytes accessed | tf_op | source)
XLA Modules:
  0.0 281.4 jit_solution(8402606530868346347)
XLA Ops:
  1.3 0.1 iota.11
  1.4 0.1 iota.12
  1.5 0.1 pad.2.clone
  1.5 0.7 maximum_maximum_fusion
  2.3 0.6 broadcast_in_dim.33.refs_2_
  2.9 0.1 broadcast_in_dim.36
  3.0 0.6 broadcast_select_fusion.refs_7_
  3.6 272.1 %shard_map.152 = (bf16[512,1024]{1,0:T(8,128)(2,1)}, f32[512,1024]{1,0:T(8,128)}, bf16[512,1024]{1,0:T(8,128)(2,1)}, bf16[4,2,2,2,32,3072]{5,4,3,2,1,0:T(8,128)(...) custom-call(bf16[512,1024]{1,0:T(8,128)(2,1)} %bitcast.6, ...), custom_call_target="tpu_custom_call" | custom-call | tf_op jit(solution)/shard_map/pallas_call | solution.py:1107
  275.7 5.5 %shard_map.153 = (bf16[512,1024]{1,0:T(8,128)(2,1)}, f32[512,1024]{1,0:T(8,128)}, f32[32,3072]{1,0:T(8,128)}, f32[32,1024]{1,0:T(8,128)}, f32[32,4096]{1,0:T(8,1...) custom-call(bf16[512,1024]{1,0:T(8,128)(2,1)} %get-tuple-element.24.fo, ...), custom_call_target="tpu_custom_call" | custom-call | tf_op jit(solution)/shard_map/pallas_call | solution.py:1189
  (3 shorter events, 0.0 us)

commit v3 on v2

--- a/solution.py
+++ b/solution.py
@@ -690,12 +690,11 @@
     ag.stage(0, 0)
     ag.stage(1, 0)
     swap_start(0)
-    swap_start(5)
     ag.stage(0, 1)
     ag.tick(2)
+    swap_start(5)
+    ag.tick(3)
     swap_start(6)
-    ag.tick(3)
-    swap_start(7)
     ag.stage(0, 4)
     get_par = load(0, f_par, parv)
     get_par.start()
@@ -715,14 +714,16 @@
         h1[part, :] = (nrm * par[0:1, :] + par[2:3, :]).astype(BF)
 
     ag.tick(4)
-    swap_start(8)
-    for i in range(4):
-        swap_wait(5 + i)
-    tiles(rows // step, step, norm_one)
+    swap_start(7)
     keyvals = between(14, qkv.at[:, pl.ds(d, 2 * d)], cross)
     ag.stage(1, 4)
     for i, b in enumerate((1, 2, 0)):
         ag.tick(5 + i)
+        if i == 0:
+            swap_start(8)
+            for k in range(4):
+                swap_wait(5 + k)
+            tiles(rows // step, step, norm_one)
         ag.stage(2 + i, 4)
         get = load_block(1 + i, b)
         get.start()

time: 284 us -> 286 us (level)
  Pallas kernels: 278 us -> 281 us
    pallas_call x1, Pallas kernels: 272 us -> 276 us  [layer(): pl.pallas_call(functools.partial(layer_kernel, nz), out_shape=[S((rows, d...]
where the time goes in v3:
time: 286 us; the launch traced here: 285 us
  Pallas kernels  281 us (98%)
    pallas_call x1, Pallas kernels, layer(): pl.pallas_call(functools.partial(layer_kernel, nz), out_shape=[S((rows, d...  276 us

profile of v3, /device:TPU:0, one launch (start us, length us, event | category | flops | bytes accessed | tf_op | source)
XLA Modules:
  0.0 284.9 jit_solution(1131632586203093061)
XLA Ops:
  1.3 0.1 iota.11
  1.4 0.1 iota.12
  1.5 0.1 pad.2.clone
  1.5 0.7 maximum_maximum_fusion
  2.3 0.6 broadcast_in_dim.33.refs_2_
  2.9 0.1 broadcast_in_dim.36
  3.0 0.6 broadcast_select_fusion.refs_7_
  3.6 275.7 %shard_map.152 = (bf16[512,1024]{1,0:T(8,128)(2,1)}, f32[512,1024]{1,0:T(8,128)}, bf16[512,1024]{1,0:T(8,128)(2,1)}, bf16[4,2,2,2,32,3072]{5,4,3,2,1,0:T(8,128)(...) custom-call(bf16[512,1024]{1,0:T(8,128)(2,1)} %bitcast.6, ...), custom_call_target="tpu_custom_call" | custom-call | tf_op jit(solution)/shard_map/pallas_call | solution.py:1108
  279.3 5.5 %shard_map.153 = (bf16[512,1024]{1,0:T(8,128)(2,1)}, f32[512,1024]{1,0:T(8,128)}, f32[32,3072]{1,0:T(8,128)}, f32[32,1024]{1,0:T(8,128)}, f32[32,4096]{1,0:T(8,1...) custom-call(bf16[512,1024]{1,0:T(8,128)(2,1)} %get-tuple-element.24.fo, ...), custom_call_target="tpu_custom_call" | custom-call | tf_op jit(solution)/shard_map/pallas_call | solution.py:1190
  (3 shorter events, 0.0 us)

commit v4 on v2

--- a/solution.py
+++ b/solution.py
@@ -1026,7 +1026,7 @@
         return gp.at[2 * lax.rem(j, 2) + i // 2, i % 2, :, :, mixed_cols(j)]
 
     maker.run(
-        6, lambda j: dot_nn(row_half(j), qkv[:, mixed_cols(j)]), row_blocks, mixed_target, {1: rs_tick(9), 2: rs_begin(9), 4: rs_begin(10)}
+        6, lambda j: dot_nn(row_half(j), qkv[:, mixed_cols(j)]), row_blocks, mixed_target, {2: rs_begin(9), 3: rs_tick(9), 4: rs_begin(10)}
     )
     maker.flush()
     rs.stage(11, 0)

time: 284 us -> 281 us (0.989)
  no operation moved by 1% of the time
where the time goes in v4:
time: 281 us
  Pallas kernels  277 us (99%)
    pallas_call x1, Pallas kernels, layer(): pl.pallas_call(functools.partial(layer_kernel, nz), out_shape=[S((rows, d...  271 us

profile of v4, /device:TPU:0, one launch (start us, length us, event | category | flops | bytes accessed | tf_op | source)
XLA Modules:
  0.0 280.6 jit_solution(6833366192842078363)
XLA Ops:
  1.3 0.1 iota.11
  1.4 0.1 iota.12
  1.5 0.1 pad.2.clone
  1.5 0.7 maximum_maximum_fusion
  2.3 0.6 broadcast_in_dim.33.refs_2_
  2.9 0.1 broadcast_in_dim.36
  3.0 0.6 broadcast_select_fusion.refs_7_
  3.6 271.3 %shard_map.152 = (bf16[512,1024]{1,0:T(8,128)(2,1)}, f32[512,1024]{1,0:T(8,128)}, bf16[512,1024]{1,0:T(8,128)(2,1)}, bf16[4,2,2,2,32,3072]{5,4,3,2,1,0:T(8,128)(...) custom-call(bf16[512,1024]{1,0:T(8,128)(2,1)} %bitcast.6, ...), custom_call_target="tpu_custom_call" | custom-call | tf_op jit(solution)/shard_map/pallas_call | solution.py:1107
  274.9 5.5 %shard_map.153 = (bf16[512,1024]{1,0:T(8,128)(2,1)}, f32[512,1024]{1,0:T(8,128)}, f32[32,3072]{1,0:T(8,128)}, f32[32,1024]{1,0:T(8,128)}, f32[32,4096]{1,0:T(8,1...) custom-call(bf16[512,1024]{1,0:T(8,128)(2,1)} %get-tuple-element.24.fo, ...), custom_call_target="tpu_custom_call" | custom-call | tf_op jit(solution)/shard_map/pallas_call | solution.py:1189
  (3 shorter events, 0.0 us)
